TPU v7x, 256 devices: a whole 4x4x8 slice. The times are simulated.
256 devices in a mesh: dp: 256 (over y, z, x, core).
Axes of the slice: x: 4, y: 4, z: 8, core: 2. Of those that a mesh axis runs over, the one named last changes fastest.
Arguments:
- images: bfloat16 [1048576, 256], P('dp'), may hold values from -8 to 8
- landmarks: bfloat16 [512, 256], replicated, may hold values from -6 to 6
Outputs:
- q_factor: float32 [1048576, 512], P('dp')
- r_factor: float32 [512, 512], replicated
All inputs are finite; a program needn't handle non-finite values.
Results may differ from a plain program's by a relative error of at most 0.0003.
Values sent between devices are 32-bit elements; how exact they have to be, the bound alone decides.
A program may use at most 128 MiB of HBM per device.

v0:
```python
import functools
import math

import jax
import jax.numpy as jnp
from jax import lax
from jax.experimental import pallas as pl
from jax.experimental.pallas import tpu as pltpu
from jax.sharding import PartitionSpec as P

MESH = pl.DeviceIdType.MESH
NX, NY, NZ = 4, 4, 8
NXY = NX*NY

def dev(y, z, x, c):
    return ((y * NZ + z) * NX + x) * 2 + c

def comm_kernel(chunks, g_ref, o_ref, crecv, half, rsbuf, zbuf, part,
                c_ss, c_rs, rs_ss, rs_rs, z_ss, z_rs, ag_ss, ag_rs, f_ss, f_rs):
    me = lax.axis_index("dp")
    c = me % 2
    x = (me // 2) % NX
    z = (me // (2 * NX)) % NZ
    y = me // (2 * NX * NZ)
    sib = dev(y, z, x, 1 - c)
    def xy_peer(rel):
        px = (x + rel % NX) % NX
        py = (y + rel // NX) % NY
        return py * NX + px, dev(py, z, px, c)
    def xy_from(rel):
        px = (x + NX - rel % NX) % NX
        py = (y + NY - rel // NX) % NY
        return py * NX + px
    def z_peer(rel):
        return dev(y, (z + rel) % NZ, x, c)
    def sl(off, n):
        return pl.ds(pl.multiple_of(off, 8), n)
    bar = pltpu.get_barrier_semaphore()
    def sig(d):
        pl.semaphore_signal(bar, inc=1, device_id=(d,), device_id_type=MESH)
    sig(sib)
    @pl.loop(1, NXY)
    def _(r):
        sig(xy_peer(r)[1])
    @pl.loop(1, NZ)
    def _(r):
        sig(z_peer(r))
    pl.semaphore_wait(bar, 1 + NXY - 1 + NZ - 1)

    mine = y * NX + x
    C = []
    off = 0
    for k, rows in enumerate(chunks):
        C.append((k, off, rows // 2, rows // 32, off // 2, off // 32))
        off += rows
    def core_copy(k, off, h, p, ho, po):
        return pltpu.make_async_remote_copy(g_ref.at[sl(off + (1 - c) * h, h)], crecv.at[pl.ds(ho, h)],
            c_ss.at[k], c_rs.at[k], device_id=(sib,), device_id_type=MESH)
    def rs_copy(ch, rel):
        k, off, h, p, ho, po = ch
        idx, d = xy_peer(rel)
        return pltpu.make_async_remote_copy(half.at[sl(ho + idx * p, p)], rsbuf.at[sl(ho + rel * p, p)],
            rs_ss.at[k, rel], rs_rs.at[k, rel], device_id=(d,), device_id_type=MESH)
    def z_copy(ch, rel):
        k, off, h, p, ho, po = ch
        return pltpu.make_async_remote_copy(part.at[pl.ds(po, p)], zbuf.at[z, pl.ds(po, p)],
            z_ss.at[k, rel], z_rs.at[k, rel], device_id=(z_peer(rel),), device_id_type=MESH)
    def ag_copy(ch, rel):
        k, off, h, p, ho, po = ch
        idx, d = xy_peer(rel)
        src = o_ref.at[sl(off + c * h + mine * p, p)]
        return pltpu.make_async_remote_copy(src, src, ag_ss.at[k, rel], ag_rs.at[k, rel], device_id=(d,), device_id_type=MESH)
    def fwd_copy(ch, rel):
        k, off, h, p, ho, po = ch
        idx = xy_from(rel)
        src = o_ref.at[sl(off + c * h + idx * p, p)]
        return pltpu.make_async_remote_copy(src, src, f_ss.at[k, rel], f_rs.at[k, rel], device_id=(sib,), device_id_type=MESH)
    for ch in C:
        core_copy(*ch).start()
    for ch in C:
        k, off, h, p, ho, po = ch
        core_copy(*ch).wait_recv()
        half[pl.ds(ho, h)] = g_ref[sl(off + c * h, h)] + crecv[pl.ds(ho, h)]
        @pl.loop(1, NXY)
        def _(r):
            rs_copy(ch, r).start()
    for ch in C:
        k, off, h, p, ho, po = ch
        @pl.loop(1, NXY)
        def _(r):
            rs_copy(ch, r).wait_recv()
        acc = half[sl(ho + mine * p, p)]
        for r in range(1, NXY):
            acc = acc + rsbuf[pl.ds(ho + r * p, p)]
        part[pl.ds(po, p)] = acc
        zbuf[z, pl.ds(po, p)] = acc
        @pl.loop(1, NZ)
        def _(r):
            z_copy(ch, r).start()
    for ch in C:
        k, off, h, p, ho, po = ch
        @pl.loop(1, NZ)
        def _(r):
            z_copy(ch, r).wait_recv()
        acc = zbuf[0, pl.ds(po, p)]
        for r in range(1, NZ):
            acc = acc + zbuf[r, pl.ds(po, p)]
        o_ref[sl(off + c * h + mine * p, p)] = acc
        fwd_copy(ch, 0).start()
        @pl.loop(1, NXY)
        def _(r):
            ag_copy(ch, r).start()
    for ch in C:
        @pl.loop(1, NXY)
        def _(r):
            ag_copy(ch, r).wait_recv()
            fwd_copy(ch, r).start()
    for ch in C:
        @pl.loop(0, NXY)
        def _(r):
            k, off, h, p, ho, po = ch
            idx = xy_from(r)
            dst = o_ref.at[sl(off + (1 - c) * h + idx * p, p)]
            pltpu.make_async_remote_copy(dst, dst, f_ss.at[k, r], f_rs.at[k, r], device_id=(sib,), device_id_type=MESH).wait_recv()
    for ch in C:
        core_copy(*ch).wait_send()
        fwd_copy(ch, 0).wait_send()
        @pl.loop(1, NXY)
        def _(r):
            rs_copy(ch, r).wait_send()
            ag_copy(ch, r).wait_send()
            fwd_copy(ch, r).wait_send()
        @pl.loop(1, NZ)
        def _(r):
            z_copy(ch, r).wait_send()

def comm(g, chunks=(512, 768), cid=0):
    rows = g.shape[0]
    nc = len(chunks)
    D = pltpu.SemaphoreType.DMA
    return pl.pallas_call(
        functools.partial(comm_kernel, chunks),
        out_shape=jax.ShapeDtypeStruct((rows, 128), jnp.float32),
        in_specs=[pl.BlockSpec(memory_space=pltpu.VMEM)],
        out_specs=pl.BlockSpec(memory_space=pltpu.VMEM),
        scratch_shapes=[
            pltpu.VMEM((rows // 2, 128), jnp.float32),
            pltpu.VMEM((rows // 2, 128), jnp.float32),
            pltpu.VMEM((rows // 2, 128), jnp.float32),
            pltpu.VMEM((NZ, rows // 32, 128), jnp.float32),
            pltpu.VMEM((rows // 32, 128), jnp.float32),
            D((nc,)), D((nc,)), D((nc, NXY)), D((nc, NXY)), D((nc, NZ)), D((nc, NZ)),
            D((nc, NXY)), D((nc, NXY)), D((nc, NXY)), D((nc, NXY)),
        ],
        compiler_params=pltpu.CompilerParams(collective_id=cid, has_side_effects=True),
        name="gram_all_reduce",
    )(g)

F32 = jnp.float32
HI = lax.Precision.HIGHEST
BLK = {}
n = 0
for i in range(4):
    for j in range(i, 4):
        BLK[i, j] = n; n += 1

def mm(a, b):
    return lax.dot_general(a, b, (((1,), (0,)), ((), ())), precision=HI, preferred_element_type=F32)
def mtm(a, b):
    return lax.dot_general(a, b, (((0,), (0,)), ((), ())), precision=HI, preferred_element_type=F32)

def lane_splat(v, c):
    return jnp.broadcast_to(v[:, c:c + 1], (8, 128))
def row_splat(v, r):
    return jnp.broadcast_to(v[r:r + 1, :], (8, 128))

def tsum(xs):
    xs = list(xs)
    while len(xs) > 1:
        xs = [xs[i] + xs[i + 1] if i + 1 < len(xs) else xs[i] for i in range(0, len(xs), 2)]
    return xs[0]

def small_factor(a):
    l = [[None] * 8 for _ in range(8)]
    s = [None] * 8
    for j in range(8):
        s[j] = lax.rsqrt(a[j][j])
        for i in range(j + 1, 8):
            l[i][j] = a[i][j] * s[j]
        for i in range(j + 1, 8):
            for k in range(j + 1, i + 1):
                a[i][k] = a[i][k] - l[i][j] * l[k][j]
    w = [[None] * 8 for _ in range(8)]
    for j in range(8):
        w[j][j] = s[j]
        for i in range(j + 1, 8):
            w[i][j] = -s[i] * tsum([l[i][k] * w[k][j] for k in range(j, i)])
    return w

def diag_inverse(A):
    lane = lax.broadcasted_iota(jnp.int32, (8, 128), 1)
    sub = lax.broadcasted_iota(jnp.int32, (8, 128), 0)
    A = list(A)
    out = []
    for p in range(16):
        c0 = 8 * p
        P = A[p]
        cols = [lane_splat(P, c0 + j) for j in range(8)]
        a = [[row_splat(cols[j], i) if j <= i else None for j in range(8)] for i in range(8)]
        w = small_factor(a)
        inpanel = (lane >= c0) & (lane < c0 + 8)
        T = jnp.where(inpanel, (lane - c0 == sub).astype(F32), P)
        Tb = [row_splat(T, j) for j in range(8)]
        V = [tsum([w[i][j] * Tb[j] for j in range(i + 1)]) for i in range(8)]
        packed = V[0]
        for i in range(1, 8):
            packed = jnp.where(sub == i, V[i], packed)
        out.append(packed)
        if p < 15:
            Y = [tsum([w[i][j] * V[i] for i in range(j, 8)]) for j in range(8)]
            for q in range(p + 1, 16):
                m = [lane_splat(A[q], c0 + j) for j in range(8)]
                base = jnp.where(inpanel, 0.0, A[q])
                A[q] = base - tsum([m[j] * Y[j] for j in range(8)])
    row = [jnp.where(lane <= sub + 8 * p, out[p], 0.0) for p in range(16)]
    return row

def chol_kernel(g_ref, r_ref, hi_ref, lo_ref):
    n_rows = 1.0 / 1048576.0
    A = {k: g_ref[128 * v:128 * v + 128, :] * n_rows for k, v in BLK.items()}
    X = {}
    Bt = {}
    for k in range(4):
        strips = diag_inverse([A[k, k][8 * p:8 * p + 8, :] for p in range(16)])
        W = jnp.concatenate(strips, axis=0)
        U = {j: mm(W, A[k, j]) for j in range(k, 4)}
        for j in range(k + 1, 4):
            for i in range(k + 1, j + 1):
                A[i, j] = A[i, j] - mtm(U[i], U[j])
        X[k, k] = W
        for m in range(k):
            X[k, m] = mm(W, Bt[k, m])
        for i in range(k + 1, 4):
            for m in range(k + 1):
                t = mtm(U[i], X[k, m])
                Bt[i, m] = -t if m == k else Bt[i, m] - t
        rr = lax.broadcasted_iota(jnp.int32, (128, 128), 0)
        cc = lax.broadcasted_iota(jnp.int32, (128, 128), 1)
        for j in range(4):
            blk = jnp.zeros((128, 128), F32) if j < k else (jnp.where(rr <= cc, U[k], 0.0) if j == k else U[j])
            r_ref[128 * k:128 * k + 128, 128 * j:128 * j + 128] = blk
        for m in range(4):
            blk = X[k, m].T if m <= k else jnp.zeros((128, 128), F32)
            h = blk.astype(jnp.bfloat16)
            hi_ref[128 * m:128 * m + 128, 128 * k:128 * k + 128] = h
            lo_ref[128 * m:128 * m + 128, 128 * k:128 * k + 128] = (blk - h.astype(F32)).astype(jnp.bfloat16)

def chol(g):
    V = pl.BlockSpec(memory_space=pltpu.VMEM)
    return pl.pallas_call(chol_kernel,
        out_shape=(jax.ShapeDtypeStruct((512, 512), F32), jax.ShapeDtypeStruct((512, 512), jnp.bfloat16), jax.ShapeDtypeStruct((512, 512), jnp.bfloat16)),
        in_specs=[V], out_specs=(V, V, V),
        compiler_params=pltpu.CompilerParams(vmem_limit_bytes=40 << 20), name="factor")(g)

F32 = jnp.float32
BF = jnp.bfloat16
EPS = 1e-5
TILE = 512

def dot_t(a, b):
    return lax.dot_general(a, b, (((1,), (1,)), ((), ())), preferred_element_type=F32)
def t_dot(a, b):
    return lax.dot_general(a, b, (((0,), (0,)), ((), ())), preferred_element_type=F32)

def feat_kernel(steps, x_ref, lm_ref, ls_ref, hi_ref, lo_ref, g_ref, acc0, acc1, acc2):
    i = pl.program_id(0)
    x = x_ref[...]
    prod = dot_t(x, lm_ref[...])
    xf = x.astype(F32)
    rs = lax.rsqrt(jnp.mean(xf * xf, axis=1, keepdims=True) + EPS)
    k = jnp.exp2(prod * rs * ls_ref[0:1, :])
    hi = k.astype(BF)
    lo = (k - hi.astype(F32)).astype(BF)
    hi_ref[...] = hi
    lo_ref[...] = lo
    p0 = t_dot(hi[:, :256], jnp.concatenate([hi, lo], axis=1))
    p1 = t_dot(hi[:, 256:], jnp.concatenate([hi[:, 256:], lo[:, 256:]], axis=1))
    p2 = t_dot(lo[:, :256], hi[:, 256:])
    @pl.when(i == 0)
    def _():
        acc0[...] = p0
        acc1[...] = p1
        acc2[...] = p2
    @pl.when(i > 0)
    def _():
        acc0[...] += p0
        acc1[...] += p1
        acc2[...] += p2
    @pl.when(i == steps - 1)
    def _():
        c0 = acc0[:, 512:768]
        g00 = acc0[:, :256] + (c0 + c0.T)
        g01 = acc0[:, 256:512] + (acc0[:, 768:] + acc2[...])
        c1 = acc1[:, 256:]
        g11 = acc1[:, :256] + (c1 + c1.T)
        blocks = [g00[:128, :128], g00[:128, 128:], g01[:128, :128], g01[:128, 128:],
                  g00[128:, 128:], g01[128:, :128], g01[128:, 128:],
                  g11[:128, :128], g11[:128, 128:], g11[128:, 128:]]
        for n, b in enumerate(blocks):
            g_ref[128 * n:128 * n + 128, :] = b

def feat(x, lm, tile=TILE):
    rows = x.shape[0]
    steps = rows // tile
    lf = lm.astype(F32)
    ls = lax.rsqrt(jnp.mean(lf * lf, axis=1) + EPS) * (math.log2(math.e) / math.sqrt(x.shape[1]))
    ls = jnp.broadcast_to(ls[None, :], (8, 512))
    return pl.pallas_call(functools.partial(feat_kernel, steps), grid=(steps,),
        in_specs=[pl.BlockSpec((tile, 256), lambda i: (i, 0)), pl.BlockSpec((512, 256), lambda i: (0, 0)), pl.BlockSpec((8, 512), lambda i: (0, 0))],
        out_specs=(pl.BlockSpec((tile, 512), lambda i: (i, 0)), pl.BlockSpec((tile, 512), lambda i: (i, 0)), pl.BlockSpec((1280, 128), lambda i: (0, 0))),
        out_shape=(jax.ShapeDtypeStruct((rows, 512), BF), jax.ShapeDtypeStruct((rows, 512), BF), jax.ShapeDtypeStruct((1280, 128), F32)),
        scratch_shapes=[pltpu.VMEM((256, 1024), F32), pltpu.VMEM((256, 512), F32), pltpu.VMEM((256, 256), F32)],
        compiler_params=pltpu.CompilerParams(vmem_limit_bytes=40 << 20), name="features")(x, lm, ls)

def dot(a, b):
    return lax.dot_general(a, b, (((1,), (0,)), ((), ())), preferred_element_type=F32)

def q_kernel(hi_ref, lo_ref, rh_ref, rl_ref, q_ref):
    hi = hi_ref[...]
    lo = lo_ref[...]
    rh = rh_ref[...]
    rl = rl_ref[...]
    q_ref[:, :256] = dot(hi[:, :256], rh[:256, :256]) + (dot(hi[:, :256], rl[:256, :256]) + dot(lo[:, :256], rh[:256, :256]))
    q_ref[:, 256:] = dot(hi, rh[:, 256:]) + (dot(hi, rl[:, 256:]) + dot(lo, rh[:, 256:]))

def qmul(hi, lo, rh, rl, tile=TILE):
    rows = hi.shape[0]
    row = pl.BlockSpec((tile, 512), lambda i: (i, 0))
    whole = pl.BlockSpec((512, 512), lambda i: (0, 0))
    return pl.pallas_call(q_kernel, grid=(rows // tile,), in_specs=[row, row, whole, whole], out_specs=row,
        out_shape=jax.ShapeDtypeStruct((rows, 512), F32),
        compiler_params=pltpu.CompilerParams(vmem_limit_bytes=40 << 20), name="q_product")(hi, lo, rh, rl)


def local(images, landmarks):
    hi, lo, gram = feat(images, landmarks, 1024)
    summed = comm(gram)
    r, rh, rl = chol(summed)
    return qmul(hi, lo, rh, rl, 1024), r


def solution(mesh):
    in_specs = (P("dp", None), P())
    out_specs = (P("dp", None), P())
    return jax.shard_map(local, mesh=mesh, in_specs=in_specs, out_specs=out_specs, check_vma=False)
```

profile of v0, /device:TPU:1, one launch (start us, length us, event | category | flops | bytes accessed | tf_op | source)
XLA Modules:
  0.0 87.8 jit_solution(5534915326903465671)
XLA Ops:
  0.6 1.1 %multiply_reduce_fusion = f32[512]{0:T(512)S(1)} fusion(bf16[512,256]{1,0:T(8,128)(2,1)} %lm_ref.1), kind=kLoop, calls=%fused_computation | loop fusion | flops 392704 | bytes 264192 | tf_op jit(solution)/shard_map/reduce_sum | solution.py:316
  1.8 0.0 copy-start.5
  1.8 1.6 %copy-done.5 = bf16[4096,256]{1,0:T(8,128)(2,1)S(1)} copy-done((bf16[4096,256]{1,0:T(8,128)(2,1)S(1)}, bf16[4096,256]{1,0:T(8,128)(2,1)}, u32[]{:S(2)}) %copy-start.5) | copy-done | bytes 2097176
  3.3 0.0 copy-start.6
  3.4 0.9 %copy-done.6 = bf16[512,256]{1,0:T(8,128)(2,1)S(1)} copy-done((bf16[512,256]{1,0:T(8,128)(2,1)S(1)}, bf16[512,256]{1,0:T(8,128)(2,1)}, u32[]{:S(2)}) %copy-start.6) | copy-done | bytes 262168
  4.3 7.5 %features.1 = (bf16[4096,512]{1,0:T(8,128)(2,1)S(1)}, bf16[4096,512]{1,0:T(8,128)(2,1)S(1)}, f32[1280,128]{1,0:T(8,128)S(1)}) custom-call(bf16[4096,256]{1,0:T(8,128)(2,1)S(1)} %copy-done.5, bf16[512,256]{1,0:T(8,128)(2,1)S(1)} %copy-done.6, f32[8,512]{1,0:T(8,128)S(1)} %broadcast_in_dim.2.ls_ref), custom_call_target="tpu_custom_call" | custom-call | tf_op jit(solution)/shard_map/features/pallas_call | solution.py:318
  11.8 0.0 copy-start
  11.8 2.0 %copy-done = bf16[4096,512]{1,0:T(8,128)(2,1)} copy-done((bf16[4096,512]{1,0:T(8,128)(2,1)}, bf16[4096,512]{1,0:T(8,128)(2,1)S(1)}, u32[]{:S(2)}) %copy-start) | copy-done | bytes 4194328
  13.8 0.0 copy-start.2
  13.8 1.9 %copy-done.2 = bf16[4096,512]{1,0:T(8,128)(2,1)} copy-done((bf16[4096,512]{1,0:T(8,128)(2,1)}, bf16[4096,512]{1,0:T(8,128)(2,1)S(1)}, u32[]{:S(2)}) %copy-start.2) | copy-done | bytes 4194328
  15.7 0.0 copy-start.7
  15.7 0.8 copy-done.7
  16.6 35.7 %gram_all_reduce.1.g_ref = f32[1280,128]{1,0:T(8,128)} custom-call(f32[1280,128]{1,0:T(8,128)} %copy-done.7), custom_call_target="tpu_custom_call" | custom-call | tf_op jit(solution)/shard_map/gram_all_reduce/pallas_call | solution.py:141
  52.2 0.0 copy-start.4
  52.3 1.1 %copy-done.4 = f32[1280,128]{1,0:T(8,128)S(1)} copy-done((f32[1280,128]{1,0:T(8,128)S(1)}, f32[1280,128]{1,0:T(8,128)}, u32[]{:S(2)}) %copy-start.4) | copy-done | bytes 655384
  53.3 23.2 %factor.1 = (f32[512,512]{1,0:T(8,128)}, bf16[512,512]{1,0:T(8,128)(2,1)S(1)}, bf16[512,512]{1,0:T(8,128)(2,1)S(1)}) custom-call(f32[1280,128]{1,0:T(8,128)S(1)} %copy-done.4), custom_call_target="tpu_custom_call" | custom-call | tf_op jit(solution)/shard_map/factor/pallas_call | solution.py:260
  76.6 0.0 copy-start.1
  76.6 2.2 %copy-done.1 = bf16[4096,512]{1,0:T(8,128)(2,1)S(1)} copy-done((bf16[4096,512]{1,0:T(8,128)(2,1)S(1)}, bf16[4096,512]{1,0:T(8,128)(2,1)}, u32[]{:S(2)}) %copy-start.1) | copy-done | bytes 4194328
  78.8 0.0 copy-start.3
  78.8 2.2 %copy-done.3 = bf16[4096,512]{1,0:T(8,128)(2,1)S(1)} copy-done((bf16[4096,512]{1,0:T(8,128)(2,1)S(1)}, bf16[4096,512]{1,0:T(8,128)(2,1)}, u32[]{:S(2)}) %copy-start.3) | copy-done | bytes 4194328
  80.9 6.9 %q_product.1 = f32[4096,512]{1,0:T(8,128)} custom-call(bf16[4096,512]{1,0:T(8,128)(2,1)S(1)} %copy-done.1, bf16[4096,512]{1,0:T(8,128)(2,1)S(1)} %copy-done.3, bf16[512,512]{1,0:T(8,128)(2,1)S(1)} %get-tuple-element.11.rh_ref, bf16[512,512]{1,0:T(8,128)(2,1)S(1)} %get-tuple-element.12.rl_ref), custom_call_target="tpu_custom_call" | custom-call | tf_op jit(solution)/shard_map/q_product/pallas_call | solution.py:340
  (2 shorter events, 0.0 us)
Async XLA Ops:
  1.8 1.6 %copy-start.5 = (bf16[4096,256]{1,0:T(8,128)(2,1)S(1)}, bf16[4096,256]{1,0:T(8,128)(2,1)}, u32[]{:S(2)}) copy-start(bf16[4096,256]{1,0:T(8,128)(2,1)} %x_ref.1) | copy-start | bytes 6291460
  3.3 0.9 %copy-start.6 = (bf16[512,256]{1,0:T(8,128)(2,1)S(1)}, bf16[512,256]{1,0:T(8,128)(2,1)}, u32[]{:S(2)}) copy-start(bf16[512,256]{1,0:T(8,128)(2,1)} %lm_ref.1) | copy-start | bytes 786436
  11.8 2.0 %copy-start = (bf16[4096,512]{1,0:T(8,128)(2,1)}, bf16[4096,512]{1,0:T(8,128)(2,1)S(1)}, u32[]{:S(2)}) copy-start(bf16[4096,512]{1,0:T(8,128)(2,1)S(1)} %get-tuple-element.8.hi_ref) | copy-start | bytes 12582916
  13.8 1.9 %copy-start.2 = (bf16[4096,512]{1,0:T(8,128)(2,1)}, bf16[4096,512]{1,0:T(8,128)(2,1)S(1)}, u32[]{:S(2)}) copy-start(bf16[4096,512]{1,0:T(8,128)(2,1)S(1)} %get-tuple-element.9.lo_ref) | copy-start | bytes 12582916
  15.7 0.8 copy-start.7
  52.2 1.1 %copy-start.4 = (f32[1280,128]{1,0:T(8,128)S(1)}, f32[1280,128]{1,0:T(8,128)}, u32[]{:S(2)}) copy-start(f32[1280,128]{1,0:T(8,128)} %gram_all_reduce.1.g_ref) | copy-start | bytes 1966084
  76.6 2.2 %copy-start.1 = (bf16[4096,512]{1,0:T(8,128)(2,1)S(1)}, bf16[4096,512]{1,0:T(8,128)(2,1)}, u32[]{:S(2)}) copy-start(bf16[4096,512]{1,0:T(8,128)(2,1)} %copy-done) | copy-start | bytes 12582916
  78.8 2.2 %copy-start.3 = (bf16[4096,512]{1,0:T(8,128)(2,1)S(1)}, bf16[4096,512]{1,0:T(8,128)(2,1)}, u32[]{:S(2)}) copy-start(bf16[4096,512]{1,0:T(8,128)(2,1)} %copy-done.2) | copy-start | bytes 12582916
where the time goes:
time: 88.2 us; the launch traced here: 87.8 us
  Pallas kernels  73.3 us (83%)
  local copies, waits for them, and re-layouts  12.8 us (15%)
  other arithmetic  1.1 us (1%)
    pallas_call x1, Pallas kernels, comm(): pl.pallas_call(functools.partial(comm_kernel, chunks), out_shape=jax.Shap...  35.7 us
    pallas_call x1, Pallas kernels, chol(): pl.pallas_call(chol_kernel, out_shape=(jax.ShapeDtypeStruct((512, 512), F...  23.2 us
    unnamed x16, local copies, waits for them, and re-layouts  12.8 us
    pallas_call x1, Pallas kernels, feat(): pl.pallas_call(functools.partial(feat_kernel, steps), grid=(steps,), in_s...  7.45 us
    pallas_call x1, Pallas kernels, qmul(): pl.pallas_call(q_kernel, grid=(rows // tile,), in_specs=[row, row, whole,...  6.9 us

commit v1 on v0

v1 whole, which is shorter than its diff:
```python
import functools
import math

import jax
import jax.numpy as jnp
from jax import lax
from jax.experimental import pallas as pl
from jax.experimental.pallas import tpu as pltpu
from jax.sharding import PartitionSpec as P

F32 = jnp.float32
BF = jnp.bfloat16
EPS = 1e-5
HI = lax.Precision.HIGHEST
MESH = pl.DeviceIdType.MESH
NX, NY, NZ = 4, 4, 8
NXY = NX * NY
TILES = 4
CHUNKS = (512, 768)

def dot_t(a, b, precision=None):
    return lax.dot_general(a, b, (((1,), (1,)), ((), ())), precision=precision, preferred_element_type=F32)

def t_dot(a, b):
    return lax.dot_general(a, b, (((0,), (0,)), ((), ())), preferred_element_type=F32)

def dev(y, z, x, c):
    return ((y * NZ + z) * NX + x) * 2 + c

def gram_kernel(x_ref, lm_ref, o_ref, hi_ref, lo_ref, xbuf, hbuf, lbuf, g_ref, acc0, acc2,
                crecv, half, rsbuf, zbuf, part, x_s, h_s, l_s,
                c_ss, c_rs, rs_ss, rs_rs, z_ss, z_rs, ag_ss, ag_rs, f_ss, f_rs):
    me = lax.axis_index("dp")
    c = me % 2
    x = (me // 2) % NX
    z = (me // (2 * NX)) % NZ
    y = me // (2 * NX * NZ)
    sib = dev(y, z, x, 1 - c)
    tile = x_ref.shape[0] // TILES

    def xy_peer(rel):
        px = (x + rel % NX) % NX
        py = (y + rel // NX) % NY
        return py * NX + px, dev(py, z, px, c)

    def xy_from(rel):
        px = (x + NX - rel % NX) % NX
        py = (y + NY - rel // NX) % NY
        return py * NX + px

    def z_peer(rel):
        return dev(y, (z + rel) % NZ, x, c)

    def sl(off, n):
        return pl.ds(pl.multiple_of(off, 8), n)

    def rows(t):
        return pl.ds(t * tile, tile)

    def x_copy(t):
        return pltpu.make_async_copy(x_ref.at[rows(t)], xbuf.at[rows(t)], x_s.at[t])

    def h_copy(t):
        return pltpu.make_async_copy(hbuf.at[rows(t)], hi_ref.at[rows(t)], h_s.at[t])

    def l_copy(t):
        return pltpu.make_async_copy(lbuf.at[rows(t)], lo_ref.at[rows(t)], l_s.at[t])

    for t in range(TILES):
        x_copy(t).start()

    bar = pltpu.get_barrier_semaphore()

    def sig(d):
        pl.semaphore_signal(bar, inc=1, device_id=(d,), device_id_type=MESH)

    sig(sib)

    @pl.loop(1, NXY)
    def _(r):
        sig(xy_peer(r)[1])

    @pl.loop(1, NZ)
    def _(r):
        sig(z_peer(r))

    lf = lm_ref[...].astype(F32)
    ones = jnp.full((8, lf.shape[1]), 1.0 / lf.shape[1], F32)
    ls = lax.rsqrt(dot_t(ones, lf * lf, HI) + EPS)[0:1, :] * (math.log2(math.e) / math.sqrt(lf.shape[1]))

    def features(t):
        xt = xbuf[rows(t), :]
        xf = xt.astype(F32)
        rs = lax.rsqrt(jnp.mean(xf * xf, axis=1, keepdims=True) + EPS)
        k = jnp.exp2(dot_t(xt, lm_ref[...]) * rs * ls)
        hi = k.astype(BF)
        hbuf[rows(t), :] = hi
        lbuf[rows(t), :] = (k - hi.astype(F32)).astype(BF)

    def gram0(t):
        hi = hbuf[rows(t), :]
        lo = lbuf[rows(t), :]
        p0 = t_dot(hi[:, :256], jnp.concatenate([hi, lo], axis=1))
        p2 = t_dot(lo[:, :256], hi[:, 256:])
        if t == 0:
            acc0[...] = p0
            acc2[...] = p2
        else:
            acc0[...] += p0
            acc2[...] += p2

    for t in range(TILES + 1):
        if t < TILES:
            x_copy(t).wait()
            features(t)
        if t > 0:
            h_copy(t - 1).start()
            l_copy(t - 1).start()
            gram0(t - 1)

    def put(n, b):
        g_ref[128 * n:128 * n + 128, :] = b

    cross = acc0[:, 512:768]
    g00 = acc0[:, :256] + (cross + cross.T)
    g01 = acc0[:, 256:512] + (acc0[:, 768:] + acc2[...])
    put(0, g00[:128, :128])
    put(1, g00[:128, 128:])
    put(2, g01[:128, :128])
    put(3, g01[:128, 128:])

    mine = y * NX + x
    C = []
    off = 0
    for k, n in enumerate(CHUNKS):
        C.append((k, off, n // 2, n // 32, off // 2, off // 32))
        off += n

    def core_copy(k, off, h, p, ho, po):
        return pltpu.make_async_remote_copy(
            g_ref.at[sl(off + (1 - c) * h, h)], crecv.at[pl.ds(ho, h)],
            c_ss.at[k], c_rs.at[k], device_id=(sib,), device_id_type=MESH)

    def rs_copy(ch, rel):
        k, off, h, p, ho, po = ch
        idx, d = xy_peer(rel)
        return pltpu.make_async_remote_copy(
            half.at[sl(ho + idx * p, p)], rsbuf.at[sl(ho + rel * p, p)],
            rs_ss.at[k, rel], rs_rs.at[k, rel], device_id=(d,), device_id_type=MESH)

    def z_copy(ch, rel):
        k, off, h, p, ho, po = ch
        return pltpu.make_async_remote_copy(
            part.at[pl.ds(po, p)], zbuf.at[z, pl.ds(po, p)],
            z_ss.at[k, rel], z_rs.at[k, rel], device_id=(z_peer(rel),), device_id_type=MESH)

    def ag_copy(ch, rel):
        k, off, h, p, ho, po = ch
        idx, d = xy_peer(rel)
        src = o_ref.at[sl(off + c * h + mine * p, p)]
        return pltpu.make_async_remote_copy(
            src, src, ag_ss.at[k, rel], ag_rs.at[k, rel], device_id=(d,), device_id_type=MESH)

    def fwd_copy(ch, rel, core):
        k, off, h, p, ho, po = ch
        src = o_ref.at[sl(off + core * h + xy_from(rel) * p, p)]
        return pltpu.make_async_remote_copy(
            src, src, f_ss.at[k, rel], f_rs.at[k, rel], device_id=(sib,), device_id_type=MESH)

    pl.semaphore_wait(bar, 1 + NXY - 1 + NZ - 1)
    core_copy(*C[0]).start()

    put(4, g00[128:, 128:])
    put(5, g01[128:, :128])
    put(6, g01[128:, 128:])
    h1 = hbuf[:, 256:]
    p1 = t_dot(h1, jnp.concatenate([h1, lbuf[:, 256:]], axis=1))
    cross = p1[:, 256:]
    g11 = p1[:, :256] + (cross + cross.T)
    put(7, g11[:128, :128])
    put(8, g11[:128, 128:])
    put(9, g11[128:, 128:])
    core_copy(*C[1]).start()

    for ch in C:
        k, off, h, p, ho, po = ch
        core_copy(*ch).wait_recv()
        half[pl.ds(ho, h)] = g_ref[sl(off + c * h, h)] + crecv[pl.ds(ho, h)]
        for r in range(1, NXY):
            rs_copy(ch, r).start()
    for ch in C:
        k, off, h, p, ho, po = ch

        @pl.loop(1, NXY)
        def _(r):
            rs_copy(ch, r).wait_recv()

        acc = half[sl(ho + mine * p, p)]
        for r in range(1, NXY):
            acc = acc + rsbuf[pl.ds(ho + r * p, p)]
        part[pl.ds(po, p)] = acc
        zbuf[z, pl.ds(po, p)] = acc
        for r in range(1, NZ):
            z_copy(ch, r).start()
    for ch in C:
        k, off, h, p, ho, po = ch

        @pl.loop(1, NZ)
        def _(r):
            z_copy(ch, r).wait_recv()

        acc = zbuf[0, pl.ds(po, p)]
        for r in range(1, NZ):
            acc = acc + zbuf[r, pl.ds(po, p)]
        o_ref[sl(off + c * h + mine * p, p)] = acc
        for r in range(1, NXY):
            ag_copy(ch, r).start()
        fwd_copy(ch, 0, c).start()
    for ch in C:
        @pl.loop(1, NXY)
        def _(r):
            ag_copy(ch, r).wait_recv()
            fwd_copy(ch, r, c).start()
    for ch in C:
        @pl.loop(0, NXY)
        def _(r):
            fwd_copy(ch, r, 1 - c).wait_recv()
    for ch in C:
        core_copy(*ch).wait_send()
        fwd_copy(ch, 0, c).wait_send()

        @pl.loop(1, NXY)
        def _(r):
            rs_copy(ch, r).wait_send()
            ag_copy(ch, r).wait_send()
            fwd_copy(ch, r, c).wait_send()

        @pl.loop(1, NZ)
        def _(r):
            z_copy(ch, r).wait_send()
    for t in range(TILES):
        h_copy(t).wait()
        l_copy(t).wait()

def gram_sum(x, lm):
    rows = x.shape[0]
    g = sum(CHUNKS)
    nc = len(CHUNKS)
    D = pltpu.SemaphoreType.DMA
    VM = pltpu.VMEM
    return pl.pallas_call(
        gram_kernel,
        out_shape=(jax.ShapeDtypeStruct((g, 128), F32), jax.ShapeDtypeStruct((rows, 512), BF), jax.ShapeDtypeStruct((rows, 512), BF)),
        in_specs=[pl.BlockSpec(memory_space=pl.ANY), pl.BlockSpec(memory_space=VM)],
        out_specs=(pl.BlockSpec(memory_space=VM), pl.BlockSpec(memory_space=pl.ANY), pl.BlockSpec(memory_space=pl.ANY)),
        scratch_shapes=[
            VM((rows, 256), BF), VM((rows, 512), BF), VM((rows, 512), BF), VM((g, 128), F32),
            VM((256, 1024), F32), VM((256, 256), F32),
            VM((g // 2, 128), F32), VM((g // 2, 128), F32), VM((g // 2, 128), F32),
            VM((NZ, g // 32, 128), F32), VM((g // 32, 128), F32),
            D((TILES,)), D((TILES,)), D((TILES,)),
            D((nc,)), D((nc,)), D((nc, NXY)), D((nc, NXY)), D((nc, NZ)), D((nc, NZ)),
            D((nc, NXY)), D((nc, NXY)), D((nc, NXY)), D((nc, NXY)),
        ],
        compiler_params=pltpu.CompilerParams(collective_id=0, has_side_effects=True, vmem_limit_bytes=56 << 20),
        name="gram_sum",
    )(x, lm)

HI = jax.lax.Precision.HIGHEST
F32 = jnp.float32

BLK = {}
n = 0
for i in range(4):
    for j in range(i, 4):
        BLK[i, j] = n; n += 1

def mm(a, b):
    return lax.dot_general(a, b, (((1,), (0,)), ((), ())), precision=HI, preferred_element_type=F32)
def mtm(a, b):
    return lax.dot_general(a, b, (((0,), (0,)), ((), ())), precision=HI, preferred_element_type=F32)

def lane_splat(v, c):
    return jnp.broadcast_to(v[:, c:c + 1], (8, 128))
def row_splat(v, r):
    return jnp.broadcast_to(v[r:r + 1, :], (8, 128))

def tsum(xs):
    xs = list(xs)
    while len(xs) > 1:
        xs = [xs[i] + xs[i + 1] if i + 1 < len(xs) else xs[i] for i in range(0, len(xs), 2)]
    return xs[0]

def small_factor(a):
    l = [[None] * 8 for _ in range(8)]
    s = [None] * 8
    for j in range(8):
        s[j] = lax.rsqrt(a[j][j])
        for i in range(j + 1, 8):
            l[i][j] = a[i][j] * s[j]
        for i in range(j + 1, 8):
            for k in range(j + 1, i + 1):
                a[i][k] = a[i][k] - l[i][j] * l[k][j]
    w = [[None] * 8 for _ in range(8)]
    for j in range(8):
        w[j][j] = s[j]
        for i in range(j + 1, 8):
            w[i][j] = -s[i] * tsum([l[i][k] * w[k][j] for k in range(j, i)])
    return w

def diag_inverse(A):
    lane = lax.broadcasted_iota(jnp.int32, (8, 128), 1)
    sub = lax.broadcasted_iota(jnp.int32, (8, 128), 0)
    A = list(A)
    out = []
    for p in range(16):
        c0 = 8 * p
        P = A[p]
        cols = [lane_splat(P, c0 + j) for j in range(8)]
        a = [[row_splat(cols[j], i) if j <= i else None for j in range(8)] for i in range(8)]
        w = small_factor(a)
        inpanel = (lane >= c0) & (lane < c0 + 8)
        T = jnp.where(inpanel, (lane - c0 == sub).astype(F32), P)
        Tb = [row_splat(T, j) for j in range(8)]
        V = [tsum([w[i][j] * Tb[j] for j in range(i + 1)]) for i in range(8)]
        packed = V[0]
        for i in range(1, 8):
            packed = jnp.where(sub == i, V[i], packed)
        out.append(packed)
        if p < 15:
            Y = [tsum([w[i][j] * V[i] for i in range(j, 8)]) for j in range(8)]
            for q in range(p + 1, 16):
                m = [lane_splat(A[q], c0 + j) for j in range(8)]
                base = jnp.where(inpanel, 0.0, A[q])
                A[q] = base - tsum([m[j] * Y[j] for j in range(8)])
    row = [jnp.where(lane <= sub + 8 * p, out[p], 0.0) for p in range(16)]
    return row

def chol_kernel(g_ref, r_ref, hi_ref, lo_ref):
    n_rows = 1.0 / 1048576.0
    A = {k: g_ref[128 * v:128 * v + 128, :] * n_rows for k, v in BLK.items()}
    X = {}
    Bt = {}
    for k in range(4):
        strips = diag_inverse([A[k, k][8 * p:8 * p + 8, :] for p in range(16)])
        W = jnp.concatenate(strips, axis=0)
        U = {j: mm(W, A[k, j]) for j in range(k, 4)}
        for j in range(k + 1, 4):
            for i in range(k + 1, j + 1):
                A[i, j] = A[i, j] - mtm(U[i], U[j])
        X[k, k] = W
        for m in range(k):
            X[k, m] = mm(W, Bt[k, m])
        for i in range(k + 1, 4):
            for m in range(k + 1):
                t = mtm(U[i], X[k, m])
                Bt[i, m] = -t if m == k else Bt[i, m] - t
        rr = lax.broadcasted_iota(jnp.int32, (128, 128), 0)
        cc = lax.broadcasted_iota(jnp.int32, (128, 128), 1)
        for j in range(4):
            blk = jnp.zeros((128, 128), F32) if j < k else (jnp.where(rr <= cc, U[k], 0.0) if j == k else U[j])
            r_ref[128 * k:128 * k + 128, 128 * j:128 * j + 128] = blk
        for m in range(4):
            blk = X[k, m].T if m <= k else jnp.zeros((128, 128), F32)
            h = blk.astype(jnp.bfloat16)
            hi_ref[128 * m:128 * m + 128, 128 * k:128 * k + 128] = h
            lo_ref[128 * m:128 * m + 128, 128 * k:128 * k + 128] = (blk - h.astype(F32)).astype(jnp.bfloat16)

def chol(g):
    V = pl.BlockSpec(memory_space=pltpu.VMEM)
    return pl.pallas_call(chol_kernel,
        out_shape=(jax.ShapeDtypeStruct((512, 512), F32), jax.ShapeDtypeStruct((512, 512), jnp.bfloat16), jax.ShapeDtypeStruct((512, 512), jnp.bfloat16)),
        in_specs=[V], out_specs=(V, V, V),
        compiler_params=pltpu.CompilerParams(vmem_limit_bytes=56 << 20), name="factor")(g)

F32 = jnp.float32
def dot(a, b):
    return lax.dot_general(a, b, (((1,), (0,)), ((), ())), preferred_element_type=F32)

def q_kernel(hi_ref, lo_ref, rh_ref, rl_ref, q_ref):
    hi = hi_ref[...]
    lo = lo_ref[...]
    rh = rh_ref[...]
    rl = rl_ref[...]
    q_ref[:, :256] = dot(hi[:, :256], rh[:256, :256]) + (dot(hi[:, :256], rl[:256, :256]) + dot(lo[:, :256], rh[:256, :256]))
    q_ref[:, 256:] = dot(hi, rh[:, 256:]) + (dot(hi, rl[:, 256:]) + dot(lo, rh[:, 256:]))

def qmul(hi, lo, rh, rl, tile=1024):
    rows = hi.shape[0]
    row = pl.BlockSpec((tile, 512), lambda i: (i, 0))
    whole = pl.BlockSpec((512, 512), lambda i: (0, 0))
    return pl.pallas_call(q_kernel, grid=(rows // tile,), in_specs=[row, row, whole, whole], out_specs=row,
        out_shape=jax.ShapeDtypeStruct((rows, 512), F32),
        compiler_params=pltpu.CompilerParams(vmem_limit_bytes=56 << 20), name="q_product")(hi, lo, rh, rl)


def local(images, landmarks):
    summed, hi, lo = gram_sum(images, landmarks)
    r, rh, rl = chol(summed)
    return qmul(hi, lo, rh, rl, 1024), r


def solution(mesh):
    in_specs = (P("dp", None), P())
    out_specs = (P("dp", None), P())
    return jax.shard_map(local, mesh=mesh, in_specs=in_specs, out_specs=out_specs, check_vma=False)
```

time: 88.2 us -> 75 us (0.85)
  local copies, waits for them, and re-layouts: 12.8 us -> 0 us
  other arithmetic: 1.1 us -> 0 us
    unnamed x16 -> x0, local copies, waits for them, and re-layouts: 12.8 us -> none
    pallas_call x2 -> x1, Pallas kernels: 43.1 us -> 39.8 us  [gram_sum(): pl.pallas_call(gram_kernel, out_shape=(jax.ShapeDtypeStruct((g, 128), F32...]
    pallas_call x1, Pallas kernels: 6.9 us -> 9.81 us  [qmul(): pl.pallas_call(q_kernel, grid=(rows // tile,), in_specs=[row, row, whole,...]
    pallas_call x1, Pallas kernels: 23.2 us -> 24.5 us  [chol(): pl.pallas_call(chol_kernel, out_shape=(jax.ShapeDtypeStruct((512, 512), F...]
    reduce_sum x1 -> x0, other arithmetic: 1.1 us -> none  [feat(): jnp.mean(lf * lf, axis=1) + EPS]
where the time goes in v1:
time: 75 us; the launch traced here: 74.7 us
  Pallas kernels  74.1 us (99%)
    pallas_call x1, Pallas kernels, gram_sum(): pl.pallas_call(gram_kernel, out_shape=(jax.ShapeDtypeStruct((g, 128), F32...  39.8 us
    pallas_call x1, Pallas kernels, chol(): pl.pallas_call(chol_kernel, out_shape=(jax.ShapeDtypeStruct((512, 512), F...  24.5 us
    pallas_call x1, Pallas kernels, qmul(): pl.pallas_call(q_kernel, grid=(rows // tile,), in_specs=[row, row, whole,...  9.81 us

profile of v1, /device:TPU:1, one launch (start us, length us, event | category | flops | bytes accessed | tf_op | source)
XLA Modules:
  0.0 74.7 jit_solution(17642614032313646375)
XLA Ops:
  0.6 39.8 %gram_sum.1 = (f32[1280,128]{1,0:T(8,128)}, bf16[4096,512]{1,0:T(8,128)(2,1)}, bf16[4096,512]{1,0:T(8,128)(2,1)}) custom-call(bf16[4096,256]{1,0:T(8,128)(2,1)} %x_ref.1, bf16[512,256]{1,0:T(8,128)(2,1)} %lm_ref.1), custom_call_target="tpu_custom_call" | custom-call | tf_op jit(solution)/shard_map/gram_sum/pallas_call | solution.py:251
  40.4 24.5 %factor.1 = (f32[512,512]{1,0:T(8,128)}, bf16[512,512]{1,0:T(8,128)(2,1)}, bf16[512,512]{1,0:T(8,128)(2,1)}) custom-call(f32[1280,128]{1,0:T(8,128)} %get-tuple-element.10.g_ref), custom_call_target="tpu_custom_call" | custom-call | tf_op jit(solution)/shard_map/factor/pallas_call | solution.py:371
  64.9 9.8 %q_product.1 = f32[4096,512]{1,0:T(8,128)} custom-call(bf16[4096,512]{1,0:T(8,128)(2,1)} %get-tuple-element.8.hi_ref, bf16[4096,512]{1,0:T(8,128)(2,1)} %get-tuple-element.9.lo_ref, bf16[512,512]{1,0:T(8,128)(2,1)} %get-tuple-element.11.rh_ref, bf16[512,512]{1,0:T(8,128)(2,1)} %get-tuple-element.12.rl_ref), custom_call_target="tpu_custom_call" | custom-call | tf_op jit(solution)/shard_map/q_product/pallas_call | solution.py:392

commit v2 on v1

--- a/solution.py
+++ b/solution.py
@@ -266,22 +266,18 @@
         name="gram_sum",
     )(x, lm)
 
-HI = jax.lax.Precision.HIGHEST
 F32 = jnp.float32
-
-BLK = {}
-n = 0
-for i in range(4):
-    for j in range(i, 4):
-        BLK[i, j] = n; n += 1
+HI = lax.Precision.HIGHEST
 
 def mm(a, b):
     return lax.dot_general(a, b, (((1,), (0,)), ((), ())), precision=HI, preferred_element_type=F32)
+
 def mtm(a, b):
     return lax.dot_general(a, b, (((0,), (0,)), ((), ())), precision=HI, preferred_element_type=F32)
 
 def lane_splat(v, c):
     return jnp.broadcast_to(v[:, c:c + 1], (8, 128))
+
 def row_splat(v, r):
     return jnp.broadcast_to(v[r:r + 1, :], (8, 128))
 
@@ -291,113 +287,236 @@
         xs = [xs[i] + xs[i + 1] if i + 1 < len(xs) else xs[i] for i in range(0, len(xs), 2)]
     return xs[0]
 
-def small_factor(a):
-    l = [[None] * 8 for _ in range(8)]
-    s = [None] * 8
-    for j in range(8):
-        s[j] = lax.rsqrt(a[j][j])
-        for i in range(j + 1, 8):
-            l[i][j] = a[i][j] * s[j]
-        for i in range(j + 1, 8):
-            for k in range(j + 1, i + 1):
-                a[i][k] = a[i][k] - l[i][j] * l[k][j]
-    w = [[None] * 8 for _ in range(8)]
-    for j in range(8):
-        w[j][j] = s[j]
-        for i in range(j + 1, 8):
-            w[i][j] = -s[i] * tsum([l[i][k] * w[k][j] for k in range(j, i)])
-    return w
-
-def diag_inverse(A):
+def diag_inverse(A, between=lambda: None):
     lane = lax.broadcasted_iota(jnp.int32, (8, 128), 1)
     sub = lax.broadcasted_iota(jnp.int32, (8, 128), 0)
     A = list(A)
     out = []
+    cols = [lane_splat(A[0], j) for j in range(8)]
     for p in range(16):
         c0 = 8 * p
-        P = A[p]
-        cols = [lane_splat(P, c0 + j) for j in range(8)]
-        a = [[row_splat(cols[j], i) if j <= i else None for j in range(8)] for i in range(8)]
-        w = small_factor(a)
+        last = p == 15
         inpanel = (lane >= c0) & (lane < c0 + 8)
-        T = jnp.where(inpanel, (lane - c0 == sub).astype(F32), P)
-        Tb = [row_splat(T, j) for j in range(8)]
-        V = [tsum([w[i][j] * Tb[j] for j in range(i + 1)]) for i in range(8)]
-        packed = V[0]
+        if not last:
+            mk = [lane_splat(A[p + 1], c0 + j) for j in range(8)]
+            raw = list(mk)
+            nxt = [lane_splat(A[p + 1], c0 + 8 + j) for j in range(8)]
+        D = cols
+        Wc = [None] * 8
+        r = [None] * 8
+        piv = [None] * 8
+        for j in range(8):
+            piv[j] = row_splat(D[j], j)
+            r[j] = 1.0 / piv[j]
+            f = D[j] * r[j]
+            e = [row_splat(D[j], k) for k in range(8)]
+            for k in range(j + 1, 8):
+                D[k] = D[k] - f * e[k]
+            if not last:
+                f2 = mk[j] * r[j]
+                for k in range(j + 1, 8):
+                    mk[k] = mk[k] - f2 * e[k]
+                for k in range(8):
+                    nxt[k] = nxt[k] - f2 * row_splat(mk[j], k)
+            fm = jnp.where(sub > j, f, 0.0)
+            for k in range(j):
+                Wc[k] = Wc[k] - fm * row_splat(Wc[k], j)
+            Wc[j] = jnp.where(sub == j, 1.0, -fm)
+        pv = piv[0]
         for i in range(1, 8):
-            packed = jnp.where(sub == i, V[i], packed)
-        out.append(packed)
-        if p < 15:
-            Y = [tsum([w[i][j] * V[i] for i in range(j, 8)]) for j in range(8)]
+            pv = jnp.where(sub == i, piv[i], pv)
+        T = jnp.where(inpanel, (lane - c0 == sub).astype(F32), A[p])
+        V = tsum([Wc[j] * row_splat(T, j) for j in range(8)])
+        out.append(jnp.where(lane <= sub + c0, V * lax.rsqrt(pv), 0.0))
+        if not last:
+            Vb = [row_splat(V, s) * r[s] for s in range(8)]
+            Y = [tsum([Vb[k]] + [row_splat(Wc[k], s) * Vb[s] for s in range(k + 1, 8)]) for k in range(8)]
             for q in range(p + 1, 16):
-                m = [lane_splat(A[q], c0 + j) for j in range(8)]
+                m = raw if q == p + 1 else [lane_splat(A[q], c0 + j) for j in range(8)]
                 base = jnp.where(inpanel, 0.0, A[q])
                 A[q] = base - tsum([m[j] * Y[j] for j in range(8)])
-    row = [jnp.where(lane <= sub + 8 * p, out[p], 0.0) for p in range(16)]
-    return row
-
-def chol_kernel(g_ref, r_ref, hi_ref, lo_ref):
-    n_rows = 1.0 / 1048576.0
-    A = {k: g_ref[128 * v:128 * v + 128, :] * n_rows for k, v in BLK.items()}
-    X = {}
-    Bt = {}
+            cols = nxt
+        between()
+    return out
+
+QT = 512
+QS = 128
+
+def factor_kernel(g_ref, hi_ref, lo_ref, q_ref, r_ref, hb, lb, qb, rb, rh, rl, in_s, q0_s, q1_s, r_s):
+    rows = hi_ref.shape[0]
+    nt = rows // QT
+
+    def loads(t):
+        s = pl.ds(t * QT, QT)
+        return (pltpu.make_async_copy(hi_ref.at[s], hb.at[s], in_s.at[0, t]),
+                pltpu.make_async_copy(lo_ref.at[s], lb.at[s], in_s.at[1, t]))
+
+    def q_out(t, half, sem):
+        s = pl.ds(t * QT, QT)
+        cols = pl.ds(256 * half, 256)
+        return pltpu.make_async_copy(qb.at[s, cols], q_ref.at[s, cols], sem.at[t])
+
+    def r_out(k):
+        s = pl.ds(128 * k, 128)
+        return pltpu.make_async_copy(rb.at[s], r_ref.at[s], r_s.at[k])
+
+    for t in range(nt):
+        for cp in loads(t):
+            cp.start()
+
+    order = [(i, j) for i in range(4) for j in range(i, 4)]
+    A = {ij: g_ref[128 * n:128 * n + 128, :] * (1.0 / 1048576.0) for n, ij in enumerate(order)}
+    U, X, B = {}, {}, {}
+    rr = lax.broadcasted_iota(jnp.int32, (128, 128), 0)
+    cc = lax.broadcasted_iota(jnp.int32, (128, 128), 1)
+    zero = jnp.zeros((128, 128), F32)
+    cat = jnp.concatenate
+
+    def put_inverse(k, m):
+        blk = X[k, m].T
+        h = blk.astype(jnp.bfloat16)
+        at = (slice(128 * m, 128 * m + 128), slice(128 * k, 128 * k + 128))
+        rh[at] = h
+        rl[at] = (blk - h.astype(F32)).astype(jnp.bfloat16)
+
+    def row_rest(k):
+        if k < 2:
+            w = mm(X[k, k], cat([A[k, j] for j in range(k + 2, 4)], axis=1))
+            for n, j in enumerate(range(k + 2, 4)):
+                U[k, j] = w[:, 128 * n:128 * n + 128]
+
+    def row_store(k):
+        U[k, k] = jnp.where(rr <= cc, mm(X[k, k], A[k, k]), 0.0)
+        for j in range(4):
+            rb[128 * k:128 * k + 128, 128 * j:128 * j + 128] = U[k, j] if j >= k else zero
+        r_out(k).start()
+
+    def update(k, i, js):
+        w = mtm(U[k, i], cat([U[k, j] for j in js], axis=1))
+        for n, j in enumerate(js):
+            A[i, j] = A[i, j] - w[:, 128 * n:128 * n + 128]
+
+    def inverse_row(k):
+        if k > 0:
+            w = mm(X[k, k], cat([B[k, m] for m in range(k)], axis=1))
+            for m in range(k):
+                X[k, m] = w[:, 128 * m:128 * m + 128]
+
+    def inverse_update(k, i):
+        w = mtm(U[k, i], cat([X[k, m] for m in range(k + 1)], axis=1))
+        for m in range(k + 1):
+            t = w[:, 128 * m:128 * m + 128]
+            B[i, m] = -t if m == k else B[i, m] - t
+
+    def weights(half):
+        n = 256 * (half + 1)
+        cols = slice(256 * half, 256 * half + 256)
+        h = rh[:n, cols]
+        return cat([h, rl[:n, cols], h], axis=0)
+
+    def product(row, size, half, w):
+        n = 256 * (half + 1)
+        s = slice(row, row + size)
+        h = hb[s, :n]
+        qb[s, 256 * half:256 * half + 256] = lax.dot_general(
+            cat([h, h, lb[s, :n]], axis=1), w, (((1,), (0,)), ((), ())), preferred_element_type=F32)
+
+    tasks = []
+    rate = [1]
+
+    def between():
+        for _ in range(rate[0]):
+            if tasks:
+                tasks.pop(0)()
+
+    def drain():
+        while tasks:
+            tasks.pop(0)()
+
+    def q_task(row):
+        product(row, QS, 0, W0[0])
+        if (row + QS) % QT == 0:
+            q_out(row // QT, 0, q0_s).start()
+
+    W0 = []
+    Pt = functools.partial
+    first_q = []
     for k in range(4):
-        strips = diag_inverse([A[k, k][8 * p:8 * p + 8, :] for p in range(16)])
-        W = jnp.concatenate(strips, axis=0)
-        U = {j: mm(W, A[k, j]) for j in range(k, 4)}
-        for j in range(k + 1, 4):
-            for i in range(k + 1, j + 1):
-                A[i, j] = A[i, j] - mtm(U[i], U[j])
-        X[k, k] = W
-        for m in range(k):
-            X[k, m] = mm(W, Bt[k, m])
+        strips = diag_inverse([A[k, k][8 * p:8 * p + 8, :] for p in range(16)], between)
+        if k < 2:
+            drain()
+        X[k, k] = cat(strips, axis=0)
+        if k < 3:
+            U[k, k + 1] = mm(X[k, k], A[k, k + 1])
+            update(k, k + 1, [k + 1])
+        new = []
+        if k < 3:
+            if k < 2:
+                new.append(Pt(row_rest, k))
+            for i in range(k + 1, 4):
+                js = [j for j in range(i, 4) if (i, j) != (k + 1, k + 1)]
+                if js:
+                    new.append(Pt(update, k, i, js))
+        new.append(Pt(inverse_row, k))
         for i in range(k + 1, 4):
-            for m in range(k + 1):
-                t = mtm(U[i], X[k, m])
-                Bt[i, m] = -t if m == k else Bt[i, m] - t
-        rr = lax.broadcasted_iota(jnp.int32, (128, 128), 0)
-        cc = lax.broadcasted_iota(jnp.int32, (128, 128), 1)
-        for j in range(4):
-            blk = jnp.zeros((128, 128), F32) if j < k else (jnp.where(rr <= cc, U[k], 0.0) if j == k else U[j])
-            r_ref[128 * k:128 * k + 128, 128 * j:128 * j + 128] = blk
-        for m in range(4):
-            blk = X[k, m].T if m <= k else jnp.zeros((128, 128), F32)
-            h = blk.astype(jnp.bfloat16)
-            hi_ref[128 * m:128 * m + 128, 128 * k:128 * k + 128] = h
-            lo_ref[128 * m:128 * m + 128, 128 * k:128 * k + 128] = (blk - h.astype(F32)).astype(jnp.bfloat16)
-
-def chol(g):
-    V = pl.BlockSpec(memory_space=pltpu.VMEM)
-    return pl.pallas_call(chol_kernel,
-        out_shape=(jax.ShapeDtypeStruct((512, 512), F32), jax.ShapeDtypeStruct((512, 512), jnp.bfloat16), jax.ShapeDtypeStruct((512, 512), jnp.bfloat16)),
-        in_specs=[V], out_specs=(V, V, V),
-        compiler_params=pltpu.CompilerParams(vmem_limit_bytes=56 << 20), name="factor")(g)
-
-F32 = jnp.float32
-def dot(a, b):
-    return lax.dot_general(a, b, (((1,), (0,)), ((), ())), preferred_element_type=F32)
-
-def q_kernel(hi_ref, lo_ref, rh_ref, rl_ref, q_ref):
-    hi = hi_ref[...]
-    lo = lo_ref[...]
-    rh = rh_ref[...]
-    rl = rl_ref[...]
-    q_ref[:, :256] = dot(hi[:, :256], rh[:256, :256]) + (dot(hi[:, :256], rl[:256, :256]) + dot(lo[:, :256], rh[:256, :256]))
-    q_ref[:, 256:] = dot(hi, rh[:, 256:]) + (dot(hi, rl[:, 256:]) + dot(lo, rh[:, 256:]))
-
-def qmul(hi, lo, rh, rl, tile=1024):
+            new.append(Pt(inverse_update, k, i))
+        for m in range(k + 1):
+            new.append(Pt(put_inverse, k, m))
+        new.append(Pt(row_store, k))
+        if k < 3:
+            if k == 1:
+                for f in new:
+                    f()
+                rh[256:, :256] = jnp.zeros((256, 256), jnp.bfloat16)
+                rl[256:, :256] = jnp.zeros((256, 256), jnp.bfloat16)
+                rh[128:256, :128] = jnp.zeros((128, 128), jnp.bfloat16)
+                rl[128:256, :128] = jnp.zeros((128, 128), jnp.bfloat16)
+                rh[384:, 256:384] = jnp.zeros((128, 128), jnp.bfloat16)
+                rl[384:, 256:384] = jnp.zeros((128, 128), jnp.bfloat16)
+                for t in range(nt):
+                    for cp in loads(t):
+                        cp.wait()
+                W0.append(weights(0))
+                first_q = [Pt(q_task, s) for s in range(0, rows, QS)]
+                tasks.extend(first_q)
+            elif k == 2:
+                tasks[0:0] = new
+                rate[0] = 2
+            else:
+                tasks.extend(new)
+        else:
+            drain()
+            for f in new:
+                f()
+    w = weights(1)
+    for t in range(nt):
+        product(t * QT, QT, 1, w)
+        q_out(t, 1, q1_s).start()
+    for t in range(nt):
+        q_out(t, 0, q0_s).wait()
+        q_out(t, 1, q1_s).wait()
+    for k in range(4):
+        r_out(k).wait()
+
+def factor_q(g, hi, lo):
     rows = hi.shape[0]
-    row = pl.BlockSpec((tile, 512), lambda i: (i, 0))
-    whole = pl.BlockSpec((512, 512), lambda i: (0, 0))
-    return pl.pallas_call(q_kernel, grid=(rows // tile,), in_specs=[row, row, whole, whole], out_specs=row,
-        out_shape=jax.ShapeDtypeStruct((rows, 512), F32),
-        compiler_params=pltpu.CompilerParams(vmem_limit_bytes=56 << 20), name="q_product")(hi, lo, rh, rl)
+    V = pltpu.VMEM
+    D = pltpu.SemaphoreType.DMA
+    nt = rows // QT
+    BF16 = jnp.bfloat16
+    anym = pl.BlockSpec(memory_space=pl.ANY)
+    return pl.pallas_call(
+        factor_kernel,
+        out_shape=(jax.ShapeDtypeStruct((rows, 512), F32), jax.ShapeDtypeStruct((512, 512), F32)),
+        in_specs=[pl.BlockSpec(memory_space=V), anym, anym], out_specs=(anym, anym),
+        scratch_shapes=[V((rows, 512), BF16), V((rows, 512), BF16), V((rows, 512), F32), V((512, 512), F32),
+                        V((512, 512), BF16), V((512, 512), BF16), D((2, nt)), D((nt,)), D((nt,)), D((4,))],
+        compiler_params=pltpu.CompilerParams(vmem_limit_bytes=56 << 20), name="factor_q")(g, hi, lo)
 
 
 def local(images, landmarks):
     summed, hi, lo = gram_sum(images, landmarks)
-    r, rh, rl = chol(summed)
-    return qmul(hi, lo, rh, rl, 1024), r
+    return factor_q(summed, hi, lo)
 
 
 def solution(mesh):

time: 75 us -> 64.7 us (0.86)
  Pallas kernels: 74.1 us -> 63.7 us
    pallas_call x2 -> x1, Pallas kernels: 34.3 us -> 23.9 us  [factor_q(): pl.pallas_call(factor_kernel, out_shape=(jax.ShapeDtypeStruct((rows, 512)...]
where the time goes in v2:
time: 64.7 us; the launch traced here: 64.5 us
  Pallas kernels  63.7 us (98%)
  between operations  0.82 us (1%)
    pallas_call x1, Pallas kernels, gram_sum(): pl.pallas_call(gram_kernel, out_shape=(jax.ShapeDtypeStruct((g, 128), F32...  39.8 us
    pallas_call x1, Pallas kernels, factor_q(): pl.pallas_call(factor_kernel, out_shape=(jax.ShapeDtypeStruct((rows, 512)...  23.9 us

profile of v2, /device:TPU:1, one launch (start us, length us, event | category | flops | bytes accessed | tf_op | source)
XLA Modules:
  0.0 64.5 jit_solution(15185014988435218678)
XLA Ops:
  0.6 39.8 %gram_sum.1 = (f32[1280,128]{1,0:T(8,128)}, bf16[4096,512]{1,0:T(8,128)(2,1)}, bf16[4096,512]{1,0:T(8,128)(2,1)}) custom-call(bf16[4096,256]{1,0:T(8,128)(2,1)} %x_ref.1, bf16[512,256]{1,0:T(8,128)(2,1)} %lm_ref.1), custom_call_target="tpu_custom_call" | custom-call | tf_op jit(solution)/shard_map/gram_sum/pallas_call | solution.py:251
  40.4 23.9 %factor_q.1 = (f32[4096,512]{1,0:T(8,128)}, f32[512,512]{1,0:T(8,128)}) custom-call(f32[1280,128]{1,0:T(8,128)} %get-tuple-element.5.g_ref, bf16[4096,512]{1,0:T(8,128)(2,1)} %get-tuple-element.6.hi_ref, bf16[4096,512]{1,0:T(8,128)(2,1)} %get-tuple-element.7.lo_ref), custom_call_target="tpu_custom_call" | custom-call | tf_op jit(solution)/shard_map/factor_q/pallas_call | solution.py:508

commit v3 on v2

v3 whole, which is shorter than its diff:
```python
import functools
import math

import jax
import jax.numpy as jnp
from jax import lax
from jax.experimental import pallas as pl
from jax.experimental.pallas import tpu as pltpu
from jax.sharding import PartitionSpec as P

F32 = jnp.float32
HI = lax.Precision.HIGHEST

def mm(a, b):
    return lax.dot_general(a, b, (((1,), (0,)), ((), ())), precision=HI, preferred_element_type=F32)

def mtm(a, b):
    return lax.dot_general(a, b, (((0,), (0,)), ((), ())), precision=HI, preferred_element_type=F32)

def lane_splat(v, c):
    return jnp.broadcast_to(v[:, c:c + 1], (8, 128))

def row_splat(v, r):
    return jnp.broadcast_to(v[r:r + 1, :], (8, 128))

def tsum(xs):
    xs = list(xs)
    while len(xs) > 1:
        xs = [xs[i] + xs[i + 1] if i + 1 < len(xs) else xs[i] for i in range(0, len(xs), 2)]
    return xs[0]

def diag_inverse(A, between=lambda: None):
    lane = lax.broadcasted_iota(jnp.int32, (8, 128), 1)
    sub = lax.broadcasted_iota(jnp.int32, (8, 128), 0)
    A = list(A)
    out = []
    cols = [lane_splat(A[0], j) for j in range(8)]
    for p in range(16):
        c0 = 8 * p
        last = p == 15
        inpanel = (lane >= c0) & (lane < c0 + 8)
        if not last:
            mk = [lane_splat(A[p + 1], c0 + j) for j in range(8)]
            raw = list(mk)
            nxt = [lane_splat(A[p + 1], c0 + 8 + j) for j in range(8)]
        D = cols
        Wc = [None] * 8
        r = [None] * 8
        piv = [None] * 8
        for j in range(8):
            piv[j] = row_splat(D[j], j)
            r[j] = 1.0 / piv[j]
            f = D[j] * r[j]
            e = [row_splat(D[j], k) for k in range(8)]
            for k in range(j + 1, 8):
                D[k] = D[k] - f * e[k]
            if not last:
                f2 = mk[j] * r[j]
                for k in range(j + 1, 8):
                    mk[k] = mk[k] - f2 * e[k]
                for k in range(8):
                    nxt[k] = nxt[k] - f2 * row_splat(mk[j], k)
            fm = jnp.where(sub > j, f, 0.0)
            for k in range(j):
                Wc[k] = Wc[k] - fm * row_splat(Wc[k], j)
            Wc[j] = jnp.where(sub == j, 1.0, -fm)
        pv = piv[0]
        for i in range(1, 8):
            pv = jnp.where(sub == i, piv[i], pv)
        T = jnp.where(inpanel, (lane - c0 == sub).astype(F32), A[p])
        V = tsum([Wc[j] * row_splat(T, j) for j in range(8)])
        out.append(jnp.where(lane <= sub + c0, V * lax.rsqrt(pv), 0.0))
        if not last:
            Vb = [row_splat(V, s) * r[s] for s in range(8)]
            Y = [tsum([Vb[k]] + [row_splat(Wc[k], s) * Vb[s] for s in range(k + 1, 8)]) for k in range(8)]
            for q in range(p + 1, 16):
                m = raw if q == p + 1 else [lane_splat(A[q], c0 + j) for j in range(8)]
                base = jnp.where(inpanel, 0.0, A[q])
                A[q] = base - tsum([m[j] * Y[j] for j in range(8)])
            cols = nxt
        between()
    return out

F32 = jnp.float32
BF = jnp.bfloat16
EPS = 1e-5
HI = lax.Precision.HIGHEST
MESH = pl.DeviceIdType.MESH
NX, NY, NZ = 4, 4, 8
NXY = NX * NY
TILES = 8
CHUNKS = (512, 768)

def dot_t(a, b, precision=None):
    return lax.dot_general(a, b, (((1,), (1,)), ((), ())), precision=precision, preferred_element_type=F32)

def t_dot(a, b):
    return lax.dot_general(a, b, (((0,), (0,)), ((), ())), preferred_element_type=F32)

def dev(y, z, x, c):
    return ((y * NZ + z) * NX + x) * 2 + c

def gram_kernel(x_ref, l_ref, o_ref, w_ref, hi_ref, lo_ref, lm_ref, xbuf, hbuf, lbuf, g_ref, acc0, acc2,
                crecv, half, rsbuf, zbuf, part, lm_s, x_s, h_s, l_s,
                c_ss, c_rs, rs_ss, rs_rs, z_ss, z_rs, ag_ss, ag_rs, f_ss, f_rs):
    me = lax.axis_index("dp")
    c = me % 2
    x = (me // 2) % NX
    z = (me // (2 * NX)) % NZ
    y = me // (2 * NX * NZ)
    sib = dev(y, z, x, 1 - c)
    tile = x_ref.shape[0] // TILES

    def xy_peer(rel):
        px = (x + rel % NX) % NX
        py = (y + rel // NX) % NY
        return py * NX + px, dev(py, z, px, c)

    def xy_from(rel):
        px = (x + NX - rel % NX) % NX
        py = (y + NY - rel // NX) % NY
        return py * NX + px

    def z_peer(rel):
        return dev(y, (z + rel) % NZ, x, c)

    def sl(off, n):
        return pl.ds(pl.multiple_of(off, 8), n)

    def rows(t):
        return pl.ds(t * tile, tile)

    def x_copy(t):
        return pltpu.make_async_copy(x_ref.at[rows(t)], xbuf.at[rows(t)], x_s.at[t])

    def h_copy(t):
        return pltpu.make_async_copy(hbuf.at[rows(t)], hi_ref.at[rows(t)], h_s.at[t])

    def l_copy(t):
        return pltpu.make_async_copy(lbuf.at[rows(t)], lo_ref.at[rows(t)], l_s.at[t])

    lm_copy = pltpu.make_async_copy(l_ref, lm_ref, lm_s)
    lm_copy.start()
    for t in range(TILES):
        x_copy(t).start()

    bar = pltpu.get_barrier_semaphore()

    def sig(d):
        pl.semaphore_signal(bar, inc=1, device_id=(d,), device_id_type=MESH)

    sig(sib)

    @pl.loop(1, NXY)
    def _(r):
        sig(xy_peer(r)[1])

    @pl.loop(1, NZ)
    def _(r):
        sig(z_peer(r))

    lm_copy.wait()
    lf = lm_ref[...].astype(F32)
    sq = lf * lf
    sq_hi = sq.astype(BF)
    ones = jnp.full((8, lf.shape[1]), 1.0, BF)
    total = dot_t(ones, sq_hi) + dot_t(ones, (sq - sq_hi.astype(F32)).astype(BF))
    ls = lax.rsqrt(total / lf.shape[1] + EPS)[0:1, :] * (math.log2(math.e) / math.sqrt(lf.shape[1]))

    def features(t):
        xt = xbuf[rows(t), :]
        xf = xt.astype(F32)
        rs = lax.rsqrt(jnp.mean(xf * xf, axis=1, keepdims=True) + EPS)
        k = jnp.exp2(dot_t(xt, lm_ref[...]) * rs * ls)
        hi = k.astype(BF)
        hbuf[rows(t), :] = hi
        lbuf[rows(t), :] = (k - hi.astype(F32)).astype(BF)

    def gram0(t):
        hi = hbuf[rows(t), :]
        lo = lbuf[rows(t), :]
        p0 = t_dot(hi[:, :256], jnp.concatenate([hi, lo], axis=1))
        p2 = t_dot(lo[:, :256], hi[:, 256:])
        if t == 0:
            acc0[...] = p0
            acc2[...] = p2
        else:
            acc0[...] += p0
            acc2[...] += p2

    for t in range(TILES + 1):
        if t < TILES:
            x_copy(t).wait()
            features(t)
        if t > 0:
            h_copy(t - 1).start()
            l_copy(t - 1).start()
            gram0(t - 1)

    def put(n, b):
        g_ref[128 * n:128 * n + 128, :] = b

    cross = acc0[:, 512:768]
    g00 = acc0[:, :256] + (cross + cross.T)
    g01 = acc0[:, 256:512] + (acc0[:, 768:] + acc2[...])
    put(0, g00[:128, :128])
    put(1, g00[:128, 128:])
    put(2, g01[:128, :128])
    put(3, g01[:128, 128:])

    mine = y * NX + x
    C = []
    off = 0
    for k, n in enumerate(CHUNKS):
        C.append((k, off, n // 2, n // 32, off // 2, off // 32))
        off += n

    def core_copy(k, off, h, p, ho, po):
        return pltpu.make_async_remote_copy(
            g_ref.at[sl(off + (1 - c) * h, h)], crecv.at[pl.ds(ho, h)],
            c_ss.at[k], c_rs.at[k], device_id=(sib,), device_id_type=MESH)

    def rs_copy(ch, rel):
        k, off, h, p, ho, po = ch
        idx, d = xy_peer(rel)
        return pltpu.make_async_remote_copy(
            half.at[sl(ho + idx * p, p)], rsbuf.at[sl(ho + rel * p, p)],
            rs_ss.at[k, rel], rs_rs.at[k, rel], device_id=(d,), device_id_type=MESH)

    def z_copy(ch, rel):
        k, off, h, p, ho, po = ch
        return pltpu.make_async_remote_copy(
            part.at[pl.ds(po, p)], zbuf.at[z, pl.ds(po, p)],
            z_ss.at[k, rel], z_rs.at[k, rel], device_id=(z_peer(rel),), device_id_type=MESH)

    def ag_copy(ch, rel):
        k, off, h, p, ho, po = ch
        idx, d = xy_peer(rel)
        src = o_ref.at[sl(off + c * h + mine * p, p)]
        return pltpu.make_async_remote_copy(
            src, src, ag_ss.at[k, rel], ag_rs.at[k, rel], device_id=(d,), device_id_type=MESH)

    def fwd_copy(ch, rel, core):
        k, off, h, p, ho, po = ch
        src = o_ref.at[sl(off + core * h + xy_from(rel) * p, p)]
        return pltpu.make_async_remote_copy(
            src, src, f_ss.at[k, rel], f_rs.at[k, rel], device_id=(sib,), device_id_type=MESH)

    pl.semaphore_wait(bar, 1 + NXY - 1 + NZ - 1)
    core_copy(*C[0]).start()

    put(4, g00[128:, 128:])
    put(5, g01[128:, :128])
    put(6, g01[128:, 128:])
    h1 = hbuf[:, 256:]
    p1 = t_dot(h1, jnp.concatenate([h1, lbuf[:, 256:]], axis=1))
    cross = p1[:, 256:]
    g11 = p1[:, :256] + (cross + cross.T)
    put(7, g11[:128, :128])
    put(8, g11[:128, 128:])
    put(9, g11[128:, 128:])
    core_copy(*C[1]).start()

    for ch in C:
        k, off, h, p, ho, po = ch
        core_copy(*ch).wait_recv()
        half[pl.ds(ho, h)] = g_ref[sl(off + c * h, h)] + crecv[pl.ds(ho, h)]
        for r in range(1, NXY):
            rs_copy(ch, r).start()
    for ch in C:
        k, off, h, p, ho, po = ch

        @pl.loop(1, NXY)
        def _(r):
            rs_copy(ch, r).wait_recv()

        acc = half[sl(ho + mine * p, p)]
        for r in range(1, NXY):
            acc = acc + rsbuf[pl.ds(ho + r * p, p)]
        part[pl.ds(po, p)] = acc
        zbuf[z, pl.ds(po, p)] = acc
        for r in range(1, NZ):
            z_copy(ch, r).start()
    for ch in C:
        k, off, h, p, ho, po = ch

        @pl.loop(1, NZ)
        def _(r):
            z_copy(ch, r).wait_recv()

        acc = zbuf[0, pl.ds(po, p)]
        for r in range(1, NZ):
            acc = acc + zbuf[r, pl.ds(po, p)]
        o_ref[sl(off + c * h + mine * p, p)] = acc
        for r in range(1, NXY):
            ag_copy(ch, r).start()
        fwd_copy(ch, 0, c).start()
    @pl.loop(1, NXY)
    def _(r):
        ag_copy(C[0], r).wait_recv()
        fwd_copy(C[0], r, c).start()

    @pl.loop(0, NXY)
    def _(r):
        fwd_copy(C[0], r, 1 - c).wait_recv()

    pending = list(range(1, NXY))
    panels = [0]

    def between():
        panels[0] += 1
        while pending and panels[0] >= 8 and len(pending) > 2 * (15 - panels[0]):
            r = pending.pop(0)
            ag_copy(C[1], r).wait_recv()
            fwd_copy(C[1], r, c).start()

    first = o_ref[:128, :] * (1.0 / 1048576.0)
    w_ref[...] = jnp.concatenate(diag_inverse([first[8 * p:8 * p + 8, :] for p in range(16)], between), axis=0)

    @pl.loop(0, NXY)
    def _(r):
        fwd_copy(C[1], r, 1 - c).wait_recv()

    for ch in C:
        core_copy(*ch).wait_send()
        fwd_copy(ch, 0, c).wait_send()

        @pl.loop(1, NXY)
        def _(r):
            rs_copy(ch, r).wait_send()
            ag_copy(ch, r).wait_send()
            fwd_copy(ch, r, c).wait_send()

        @pl.loop(1, NZ)
        def _(r):
            z_copy(ch, r).wait_send()
    for t in range(TILES):
        h_copy(t).wait()
        l_copy(t).wait()

def gram_sum(x, lm):
    rows = x.shape[0]
    g = sum(CHUNKS)
    nc = len(CHUNKS)
    D = pltpu.SemaphoreType.DMA
    VM = pltpu.VMEM
    return pl.pallas_call(
        gram_kernel,
        out_shape=(jax.ShapeDtypeStruct((g, 128), F32), jax.ShapeDtypeStruct((128, 128), F32), jax.ShapeDtypeStruct((rows, 512), BF), jax.ShapeDtypeStruct((rows, 512), BF)),
        in_specs=[pl.BlockSpec(memory_space=pl.ANY), pl.BlockSpec(memory_space=pl.ANY)],
        out_specs=(pl.BlockSpec(memory_space=VM), pl.BlockSpec(memory_space=VM), pl.BlockSpec(memory_space=pl.ANY), pl.BlockSpec(memory_space=pl.ANY)),
        scratch_shapes=[
            VM((512, 256), BF), VM((rows, 256), BF), VM((rows, 512), BF), VM((rows, 512), BF), VM((g, 128), F32),
            VM((256, 1024), F32), VM((256, 256), F32),
            VM((g // 2, 128), F32), VM((g // 2, 128), F32), VM((g // 2, 128), F32),
            VM((NZ, g // 32, 128), F32), VM((g // 32, 128), F32),
            D, D((TILES,)), D((TILES,)), D((TILES,)),
            D((nc,)), D((nc,)), D((nc, NXY)), D((nc, NXY)), D((nc, NZ)), D((nc, NZ)),
            D((nc, NXY)), D((nc, NXY)), D((nc, NXY)), D((nc, NXY)),
        ],
        compiler_params=pltpu.CompilerParams(collective_id=0, has_side_effects=True, vmem_limit_bytes=56 << 20),
        name="gram_sum",
    )(x, lm)

QT = 512
QS = 128

def factor_kernel(g_ref, w_ref, hi_ref, lo_ref, q_ref, r_ref, hb, lb, qb, rb, zh, zl, w01, w23, w3, in_s, q_s, r_s):
    rows = hi_ref.shape[0]
    nt = rows // QT

    def loads(t):
        s = pl.ds(t * QT, QT)
        return (pltpu.make_async_copy(hi_ref.at[s], hb.at[s], in_s.at[0, t]),
                pltpu.make_async_copy(lo_ref.at[s], lb.at[s], in_s.at[1, t]))

    def q_out(t, part):
        s = pl.ds(t * QT, QT)
        cols = pl.ds((0, 256, 384)[part], (256, 128, 128)[part])
        return pltpu.make_async_copy(qb.at[s, cols], q_ref.at[s, cols], q_s.at[part, t])

    def r_out(k):
        s = pl.ds(128 * k, 128)
        return pltpu.make_async_copy(rb.at[s], r_ref.at[s], r_s.at[k])

    for t in range(nt):
        for cp in loads(t):
            cp.start()

    order = [(i, j) for i in range(4) for j in range(i, 4)]
    A = {ij: g_ref[128 * n:128 * n + 128, :] * (1.0 / 1048576.0) for n, ij in enumerate(order)}
    U, X, B = {}, {}, {}
    rr = lax.broadcasted_iota(jnp.int32, (128, 128), 0)
    cc = lax.broadcasted_iota(jnp.int32, (128, 128), 1)
    zero = jnp.zeros((128, 128), F32)
    cat = jnp.concatenate

    def split(blk):
        h = blk.astype(jnp.bfloat16)
        return h, (blk - h.astype(F32)).astype(jnp.bfloat16)

    def put(w, part, m, col, blk):
        h, l = split(blk)
        c = slice(col, col + 128)
        for n, v in enumerate((h, l, h)):
            w[n * part + 128 * m:n * part + 128 * m + 128, c] = v

    def row_rest(k):
        if k < 2:
            w = mm(X[k, k], cat([A[k, j] for j in range(k + 2, 4)], axis=1))
            for n, j in enumerate(range(k + 2, 4)):
                U[k, j] = w[:, 128 * n:128 * n + 128]

    def row_store(k):
        U[k, k] = jnp.where(rr <= cc, mm(X[k, k], A[k, k]), 0.0)
        for j in range(4):
            rb[128 * k:128 * k + 128, 128 * j:128 * j + 128] = U[k, j] if j >= k else zero
        r_out(k).start()

    def update(k, i, js):
        w = mtm(U[k, i], cat([U[k, j] for j in js], axis=1))
        for n, j in enumerate(js):
            A[i, j] = A[i, j] - w[:, 128 * n:128 * n + 128]

    def inverse_row(k):
        if k > 0:
            w = mm(X[k, k], cat([B[k, m] for m in range(k)], axis=1))
            for m in range(k):
                X[k, m] = w[:, 128 * m:128 * m + 128]

    def inverse_update(k, i):
        w = mtm(U[k, i], cat([X[k, m] for m in range(k + 1)], axis=1))
        for m in range(k + 1):
            t = w[:, 128 * m:128 * m + 128]
            B[i, m] = -t if m == k else B[i, m] - t

    def left(s, n):
        h = hb[s, :n]
        return cat([h, h, lb[s, :n]], axis=1)

    def dot(a, w):
        return lax.dot_general(a, w, (((1,), (0,)), ((), ())), preferred_element_type=F32)

    def done(row, part):
        if (row + QS) % QT == 0:
            q_out(row // QT, part).start()

    def q01(row):
        s = slice(row, row + QS)
        qb[s, :256] = dot(left(s, 256), w01[...])
        done(row, 0)

    def q2(row):
        s = slice(row, row + QS)
        w = dot(left(s, 384), w23[...])
        qb[s, 256:384] = w[:, :128]
        zh[s], zl[s] = split(w[:, 128:] + (hb[s, 384:].astype(F32) + lb[s, 384:].astype(F32)))
        done(row, 1)

    def q3(t):
        s = slice(t * QT, t * QT + QT)
        h = zh[s]
        qb[s, 384:] = dot(cat([h, h, zl[s]], axis=1), w3[...])
        q_out(t, 2).start()

    tasks = []
    plan = [0, 0]

    def between():
        plan[0] += 1
        while tasks and len(tasks) * 16 > plan[1] * (16 - plan[0]):
            tasks.pop(0)()

    def wait_loads():
        for t in range(nt):
            for cp in loads(t):
                cp.wait()

    def zeros():
        for n in range(3):
            w01[256 * n + 128:256 * n + 256, :128] = jnp.zeros((128, 128), jnp.bfloat16)

    Pt = functools.partial
    for k in range(4):
        plan[:] = [0, len(tasks)]
        if k == 0:
            X[0, 0] = w_ref[...]
        else:
            X[k, k] = cat(diag_inverse([A[k, k][8 * p:8 * p + 8, :] for p in range(16)], between), axis=0)
        if k < 3:
            U[k, k + 1] = mm(X[k, k], A[k, k + 1])
            update(k, k + 1, [k + 1])
        else:
            put(w3, 128, 0, 0, X[3, 3].T)
        if k < 2:
            tasks.append(Pt(row_rest, k))
        for i in range(k + 1, 4):
            js = [j for j in range(i, 4) if (i, j) != (k + 1, k + 1)]
            if js:
                tasks.append(Pt(update, k, i, js))
        if k < 3:
            tasks.append(Pt(inverse_row, k))
        for i in range(k + 1, 4):
            tasks.append(Pt(inverse_update, k, i))
        if k == 1:
            tasks.append(zeros)
            for i in range(2):
                for m in range(i + 1):
                    tasks.append(lambda i=i, m=m: put(w01, 256, m, 128 * i, X[i, m].T))
            tasks.append(wait_loads)
            tasks += [Pt(q01, s) for s in range(0, rows, QS)]
        if k == 2:
            for m in range(3):
                tasks.append(lambda m=m: put(w23, 384, m, 0, X[2, m].T))
                tasks.append(lambda m=m: put(w23, 384, m, 128, B[3, m].T))
            tasks += [Pt(q2, s) for s in range(0, rows, QS)]
        tasks.insert(len(tasks) if k < 2 else 0, Pt(row_store, k))
        if k == 3:
            for t in range(nt):
                q3(t)
            tasks.pop(0)()
    for part in range(3):
        for t in range(nt):
            q_out(t, part).wait()
    for k in range(4):
        r_out(k).wait()

def factor_q(g, w0, hi, lo):
    rows = hi.shape[0]
    V = pltpu.VMEM
    D = pltpu.SemaphoreType.DMA
    nt = rows // QT
    BF16 = jnp.bfloat16
    anym = pl.BlockSpec(memory_space=pl.ANY)
    return pl.pallas_call(
        factor_kernel,
        out_shape=(jax.ShapeDtypeStruct((rows, 512), F32), jax.ShapeDtypeStruct((512, 512), F32)),
        in_specs=[pl.BlockSpec(memory_space=V), pl.BlockSpec(memory_space=V), anym, anym], out_specs=(anym, anym),
        scratch_shapes=[V((rows, 512), BF16), V((rows, 512), BF16), V((rows, 512), F32), V((512, 512), F32),
                        V((rows, 128), BF16), V((rows, 128), BF16), V((768, 256), BF16), V((1152, 256), BF16), V((384, 128), BF16),
                        D((2, nt)), D((3, nt)), D((4,))],
        compiler_params=pltpu.CompilerParams(vmem_limit_bytes=56 << 20), name="factor_q")(g, w0, hi, lo)


def local(images, landmarks):
    summed, w0, hi, lo = gram_sum(images, landmarks)
    return factor_q(summed, w0, hi, lo)


def solution(mesh):
    in_specs = (P("dp", None), P())
    out_specs = (P("dp", None), P())
    return jax.shard_map(local, mesh=mesh, in_specs=in_specs, out_specs=out_specs, check_vma=False)
```

time: 64.7 us -> 59.8 us (0.924)
  Pallas kernels: 63.7 us -> 58.8 us
    pallas_call x1, Pallas kernels: 23.9 us -> 19.2 us  [factor_q(): pl.pallas_call(factor_kernel, out_shape=(jax.ShapeDtypeStruct((rows, 512)...]
where the time goes in v3:
time: 59.8 us; the launch traced here: 59.6 us
  Pallas kernels  58.8 us (98%)
  between operations  0.8 us (1%)
    pallas_call x1, Pallas kernels, gram_sum(): pl.pallas_call(gram_kernel, out_shape=(jax.ShapeDtypeStruct((g, 128), F32...  39.6 us
    pallas_call x1, Pallas kernels, factor_q(): pl.pallas_call(factor_kernel, out_shape=(jax.ShapeDtypeStruct((rows, 512)...  19.2 us

profile of v3, /device:TPU:1, one launch (start us, length us, event | category | flops | bytes accessed | tf_op | source)
XLA Modules:
  0.0 59.6 jit_solution(18388941294802778150)
XLA Ops:
  0.6 39.6 %gram_sum.1 = (f32[1280,128]{1,0:T(8,128)}, f32[128,128]{1,0:T(8,128)}, bf16[4096,512]{1,0:T(8,128)(2,1)}, bf16[4096,512]{1,0:T(8,128)(2,1)}) custom-call(bf16[4096,256]{1,0:T(8,128)(2,1)} %x_ref.1, bf16[512,256]{1,0:T(8,128)(2,1)} %l_ref.1), custom_call_target="tpu_custom_call" | custom-call | tf_op jit(solution)/shard_map/gram_sum/pallas_call | solution.py:347
  40.3 19.2 %factor_q.1 = (f32[4096,512]{1,0:T(8,128)}, f32[512,512]{1,0:T(8,128)}) custom-call(f32[1280,128]{1,0:T(8,128)} %get-tuple-element.6.g_ref, f32[128,128]{1,0:T(8,128)} %get-tuple-element.7.w_ref, bf16[4096,512]{1,0:T(8,128)(2,1)} %get-tuple-element.8.hi_ref, bf16[4096,512]{1,0:T(8,128)(2,1)} %get-tuple-element.9.lo_ref), custom_call_target="tpu_custom_call" | custom-call | tf_op jit(solution)/shard_map/factor_q/pallas_call | solution.py:535

commit v4 on v3

--- a/solution.py
+++ b/solution.py
@@ -295,13 +295,10 @@
         for r in range(1, NXY):
             ag_copy(ch, r).start()
         fwd_copy(ch, 0, c).start()
-    @pl.loop(1, NXY)
-    def _(r):
+    for r in (1, 3, 4, 12, 2, 5, 7, 8, 13, 15, 6, 9, 11, 14, 10):
         ag_copy(C[0], r).wait_recv()
         fwd_copy(C[0], r, c).start()
-
-    @pl.loop(0, NXY)
-    def _(r):
+    for r in range(NXY):
         fwd_copy(C[0], r, 1 - c).wait_recv()
 
     pending = list(range(1, NXY))
@@ -365,7 +362,7 @@
 QT = 512
 QS = 128
 
-def factor_kernel(g_ref, w_ref, hi_ref, lo_ref, q_ref, r_ref, hb, lb, qb, rb, zh, zl, w01, w23, w3, in_s, q_s, r_s):
+def factor_kernel(g_ref, w_ref, hi_ref, lo_ref, q_ref, r_ref, hb, lb, qb, rb, zh, zl, zh2, zl2, z3, w01, w23, w3, in_s, q_s, r_s):
     rows = hi_ref.shape[0]
     nt = rows // QT
 
@@ -447,14 +444,19 @@
 
     def q01(row):
         s = slice(row, row + QS)
-        qb[s, :256] = dot(left(s, 256), w01[...])
+        w = dot(left(s, 256), w01[...])
+        qb[s, :256] = w[:, :256]
+        rest = w[:, 256:] + (hb[s, 256:].astype(F32) + lb[s, 256:].astype(F32))
+        zh2[s], zl2[s] = split(rest[:, :128])
+        z3[s] = rest[:, 128:]
         done(row, 0)
 
     def q2(row):
         s = slice(row, row + QS)
-        w = dot(left(s, 384), w23[...])
+        h = zh2[s]
+        w = dot(cat([h, h, zl2[s]], axis=1), w23[...])
         qb[s, 256:384] = w[:, :128]
-        zh[s], zl[s] = split(w[:, 128:] + (hb[s, 384:].astype(F32) + lb[s, 384:].astype(F32)))
+        zh[s], zl[s] = split(z3[s] + w[:, 128:])
         done(row, 1)
 
     def q3(t):
@@ -498,21 +500,23 @@
             js = [j for j in range(i, 4) if (i, j) != (k + 1, k + 1)]
             if js:
                 tasks.append(Pt(update, k, i, js))
-        if k < 3:
+        if k < 2:
             tasks.append(Pt(inverse_row, k))
-        for i in range(k + 1, 4):
-            tasks.append(Pt(inverse_update, k, i))
+            for i in range(k + 1, 4):
+                tasks.append(Pt(inverse_update, k, i))
         if k == 1:
             tasks.append(zeros)
             for i in range(2):
                 for m in range(i + 1):
                     tasks.append(lambda i=i, m=m: put(w01, 256, m, 128 * i, X[i, m].T))
+            for i in range(2, 4):
+                for m in range(2):
+                    tasks.append(lambda i=i, m=m: put(w01, 256, m, 128 * i, B[i, m].T))
             tasks.append(wait_loads)
             tasks += [Pt(q01, s) for s in range(0, rows, QS)]
         if k == 2:
-            for m in range(3):
-                tasks.append(lambda m=m: put(w23, 384, m, 0, X[2, m].T))
-                tasks.append(lambda m=m: put(w23, 384, m, 128, B[3, m].T))
+            put(w23, 128, 0, 0, X[2, 2].T)
+            put(w23, 128, 0, 128, -mtm(U[2, 3], X[2, 2]).T)
             tasks += [Pt(q2, s) for s in range(0, rows, QS)]
         tasks.insert(len(tasks) if k < 2 else 0, Pt(row_store, k))
         if k == 3:
@@ -537,7 +541,8 @@
         out_shape=(jax.ShapeDtypeStruct((rows, 512), F32), jax.ShapeDtypeStruct((512, 512), F32)),
         in_specs=[pl.BlockSpec(memory_space=V), pl.BlockSpec(memory_space=V), anym, anym], out_specs=(anym, anym),
         scratch_shapes=[V((rows, 512), BF16), V((rows, 512), BF16), V((rows, 512), F32), V((512, 512), F32),
-                        V((rows, 128), BF16), V((rows, 128), BF16), V((768, 256), BF16), V((1152, 256), BF16), V((384, 128), BF16),
+                        V((rows, 128), BF16), V((rows, 128), BF16), V((rows, 128), BF16), V((rows, 128), BF16), V((rows, 128), F32),
+                        V((768, 512), BF16), V((384, 256), BF16), V((384, 128), BF16),
                         D((2, nt)), D((3, nt)), D((4,))],
         compiler_params=pltpu.CompilerParams(vmem_limit_bytes=56 << 20), name="factor_q")(g, w0, hi, lo)
 

time: 59.8 us -> 59.7 us (level)
  no operation moved by 1% of the time
where the time goes in v4:
time: 59.7 us; the launch traced here: 59.5 us
  Pallas kernels  58.8 us (98%)
  between operations  0.8 us (1%)
    pallas_call x1, Pallas kernels, gram_sum(): pl.pallas_call(gram_kernel, out_shape=(jax.ShapeDtypeStruct((g, 128), F32...  39.6 us
    pallas_call x1, Pallas kernels, factor_q(): pl.pallas_call(factor_kernel, out_shape=(jax.ShapeDtypeStruct((rows, 512)...  19.1 us

profile of v4, /device:TPU:1, one launch (start us, length us, event | category | flops | bytes accessed | tf_op | source)
XLA Modules:
  0.0 59.5 jit_solution(17605100399978511329)
XLA Ops:
  0.6 39.6 %gram_sum.1 = (f32[1280,128]{1,0:T(8,128)}, f32[128,128]{1,0:T(8,128)}, bf16[4096,512]{1,0:T(8,128)(2,1)}, bf16[4096,512]{1,0:T(8,128)(2,1)}) custom-call(bf16[4096,256]{1,0:T(8,128)(2,1)} %x_ref.1, bf16[512,256]{1,0:T(8,128)(2,1)} %l_ref.1), custom_call_target="tpu_custom_call" | custom-call | tf_op jit(solution)/shard_map/gram_sum/pallas_call | solution.py:344
  40.3 19.1 %factor_q.1 = (f32[4096,512]{1,0:T(8,128)}, f32[512,512]{1,0:T(8,128)}) custom-call(f32[1280,128]{1,0:T(8,128)} %get-tuple-element.6.g_ref, f32[128,128]{1,0:T(8,128)} %get-tuple-element.7.w_ref, bf16[4096,512]{1,0:T(8,128)(2,1)} %get-tuple-element.8.hi_ref, bf16[4096,512]{1,0:T(8,128)(2,1)} %get-tuple-element.9.lo_ref), custom_call_target="tpu_custom_call" | custom-call | tf_op jit(solution)/shard_map/factor_q/pallas_call | solution.py:539
